TPU v7x, 32 devices: a whole 2x2x4 slice. The times are simulated.
32 devices in a mesh: bond: 8 (over z, y), mpo: 4 (over x, core).
Axes of the slice: x: 2, y: 2, z: 4, core: 2. Of those that a mesh axis runs over, the one named last changes fastest.
Arguments:
- wave_blocks: bfloat16 [256, 8, 64, 256], P('bond'), may hold values from -6 to 6
- left_env: bfloat16 [256, 20, 4096], P('bond', 'mpo'), may hold values from -0.75 to 0.75
- right_env: bfloat16 [256, 20, 4096], P('bond', 'mpo'), may hold values from -0.75 to 0.75
- mpo_coef: float32 [20, 8], P('mpo'), may hold values from -3 to 3
- mpo_mask: int32 [20, 8], P('mpo'), may hold values 0 or 1
- right_sector: int32 [256, 8], replicated, may hold values from 0 to 255, as said below
Outputs:
- sigma_blocks: bfloat16 [256, 8, 64, 256], P('bond')
Inputs may be any that keep to these rules, and one draw needn't show every extreme that they name: `right_sector`: right sector b is held by bond device b // 32. The 256 blocks of the left sectors of one bond device (rows in order) name sectors of at most 64 blocks on any one bond device, and exactly 64 on some.
All inputs are finite; a program needn't handle non-finite values. No bound on the sum of `mpo_mask` on one device may be relied on, other than what follows from the above.
Results may differ from a plain program's by a relative error of at most 0.013.
Values may be sent and summed in bfloat16 or wider, within the bound.
A program may use at most 512 MiB of HBM per device.

v0:
```python
import jax
import jax.numpy as jnp
from jax import lax
from jax.sharding import PartitionSpec as P


def apply_terms(wave_rows, left_rows, right_rows):
    slot_count, block_width, column_count = wave_rows.shape
    term_count = left_rows.shape[1]
    vectors = column_count // block_width
    summed = jnp.zeros((slot_count, block_width, vectors, block_width), jnp.float32)
    for term in range(term_count):
        left_term = left_rows[:, term].reshape(slot_count, block_width, block_width)
        sectioned = jnp.einsum(
            "plk,pkc->plc", left_term, wave_rows, preferred_element_type=jnp.float32
        ).astype(jnp.bfloat16)
        right_term = right_rows[:, term].reshape(slot_count, block_width, block_width)
        summed = summed + jnp.einsum(
            "plvr,psr->plvs",
            sectioned.reshape(slot_count, block_width, vectors, block_width),
            right_term,
            preferred_element_type=jnp.float32,
        )
    return summed.reshape(slot_count, block_width, column_count).astype(jnp.bfloat16)


def route_tables(destinations, bond_index, capacity, sec_local, bond_count):
    owner_ids = destinations // sec_local
    device_ids = jnp.arange(bond_count, dtype=jnp.int32)
    owner_hits = (owner_ids[:, :, None] == device_ids[None, None, :]).astype(jnp.int32)
    earlier = jnp.cumsum(owner_hits, axis=1) - owner_hits
    slot_rank = jnp.sum(earlier * owner_hits, axis=2)
    own_slots = lax.dynamic_index_in_dim(
        owner_ids * capacity + slot_rank, bond_index, 0, keepdims=False
    )
    incoming = owner_ids == bond_index
    slot_pick = (
        (slot_rank[:, :, None] == jnp.arange(capacity, dtype=jnp.int32)[None, None, :])
        & incoming[:, :, None]
    ).astype(jnp.float32)
    local_pick = (
        (destinations % sec_local)[:, :, None]
        == jnp.arange(sec_local, dtype=jnp.int32)[None, None, :]
    ).astype(jnp.float32)
    sector_table = jnp.einsum("skr,ski->sri", slot_pick, local_pick).reshape(
        bond_count * capacity, sec_local
    )
    return (own_slots, sector_table)


def per_device(wave_blocks, left_env, right_env, mpo_coef, mpo_mask, right_sector):
    sec_local, class_count, block_width, column_count = wave_blocks.shape
    term_local = left_env.shape[1]
    blocks_local = sec_local * class_count
    bond_count = lax.axis_size("bond")
    capacity = max(1, 2 * blocks_local // bond_count)
    bond_index = lax.axis_index("bond")
    term_gains = mpo_coef * mpo_mask.astype(jnp.float32)
    wave_rows = wave_blocks.reshape(blocks_local, block_width, column_count)
    destinations = right_sector.reshape(bond_count, blocks_local)
    own_slots, sector_table = route_tables(
        destinations, bond_index, capacity, sec_local, bond_count
    )
    slot_total = bond_count * capacity
    left_scaled = (
        left_env[:, None, :, :].astype(jnp.float32) * jnp.transpose(term_gains)[None, :, :, None]
    ).astype(jnp.bfloat16)
    left_scaled = left_scaled.reshape(blocks_local, term_local, block_width * block_width)
    send_wave = (
        jnp.zeros((slot_total, block_width, column_count), jnp.bfloat16)
        .at[own_slots]
        .set(wave_rows)
    )
    send_left = (
        jnp.zeros((slot_total, term_local, block_width * block_width), jnp.bfloat16)
        .at[own_slots]
        .set(left_scaled)
    )
    right_blocks = jnp.dot(
        sector_table.astype(jnp.bfloat16),
        right_env.reshape(sec_local, -1),
        preferred_element_type=jnp.float32,
    )
    right_blocks = right_blocks.astype(jnp.bfloat16).reshape(
        slot_total, term_local, block_width * block_width
    )
    got_wave, got_left = (
        lax.all_to_all(send_wave, "bond", split_axis=0, concat_axis=0, tiled=True),
        lax.all_to_all(send_left, "bond", split_axis=0, concat_axis=0, tiled=True),
    )
    partial_sum = apply_terms(got_wave, got_left, right_blocks)
    arrived = lax.all_to_all(partial_sum, "bond", split_axis=0, concat_axis=0, tiled=True)
    returned = arrived[own_slots]
    summed = lax.psum(returned.astype(jnp.float32).astype(jnp.bfloat16), "mpo")
    return summed.reshape(wave_blocks.shape)


def solution(mesh):
    return jax.shard_map(
        per_device,
        mesh=mesh,
        in_specs=(
            P("bond", None, None, None),
            P("bond", "mpo", None),
            P("bond", "mpo", None),
            P("mpo", None),
            P("mpo", None),
            P(),
        ),
        out_specs=P("bond", None, None, None),
        check_vma=False,
    )
```

profile of v0, /device:TPU:0, one launch (start us, length us, event | category | flops | bytes accessed | tf_op | source)
XLA Modules:
  0.0 2594.4 jit_solution(17486911728146729950)
XLA Ops:
  36.1 45.2 %scatter_fusion = bf16[512,5,4096]{2,1,0:T(8,128)(2,1)} fusion(bf16[512,5,4096]{2,1,0:T(8,128)(2,1)} %broadcast_in_dim.4, s32[256]{0:T(256)S(1)} %bitcast.100, bf16[256,5,4096]{2,1,0:T(8,128)(2,1)} %fusion), kind=kCustom, calls=%fused_computation.1 | custom fusion | bytes 31458304 | tf_op jit(solution)/shard_map/scatter | solution.py:77
  94.9 37.2 %scatter_fusion.1 = bf16[512,64,256]{2,1,0:T(8,128)(2,1)} fusion(bf16[512,64,256]{2,1,0:T(8,128)(2,1)} %broadcast_in_dim.5, s32[256]{0:T(256)S(1)} %bitcast.101, bf16[256,64,256]{2,1,0:T(8,128)(2,1)} %bitcast.97), kind=kCustom, calls=%fused_computation.2 | custom fusion | bytes 25166848 | tf_op jit(solution)/shard_map/scatter | solution.py:72
  132.1 680.9 %all-to-all-done = bf16[512,5,4096]{2,1,0:T(8,128)(2,1)} async-done(((bf16[512,5,4096]{2,1,0:T(8,128)(2,1)}), bf16[512,5,4096]{2,1,0:T(8,128)(2,1)}, u32[]{:S(2)}, u32[]{:S(2)}) %all-to-all-start) | async-done | bytes 20971552 | tf_op jit(solution)/shard_map/all_to_all | solution.py:89
  829.8 28.0 %copy.61 = bf16[512,20480]{0,1:T(8,128)(2,1)} copy(bf16[512,20480]{1,0:T(8,128)(2,1)} %convolution_convert_fusion) | data formatting | bytes 41943040 | tf_op jit(solution)/shard_map/convert_element_type | solution.py:84
  937.4 92.9 %fusion.14 = (bf16[512,1,4096]{2,1,0:T(2,128)(2,1)}, bf16[512,1,4096]{2,1,0:T(2,128)(2,1)}, bf16[512,1,4096]{2,1,0:T(2,128)(2,1)}, bf16[512,1,4096]{2,1,0:T(2,128)(2,1)}, bf16[512,1,4096]{2,1,0:T(2,128)(2,1)}) fusion(bf16[512,5,4096]{2,1,0:T(8,128)(2,1)} %all-to-all-done), kind=kLoop, calls=%fused_computation.47 | loop fusion | bytes 41943040 | tf_op jit(solution)/shard_map/slice | solution.py:13
  1061.5 120.2 %all-to-all-done.1 = bf16[512,64,256]{2,1,0:T(8,128)(2,1)} async-done(((bf16[512,64,256]{2,1,0:T(8,128)(2,1)}), bf16[512,64,256]{2,1,0:T(8,128)(2,1)}, u32[]{:S(2)}, u32[]{:S(2)}) %all-to-all-start.1) | async-done | bytes 16777248 | tf_op jit(solution)/shard_map/all_to_all | solution.py:88
  1196.1 23.7 copy.58
  1219.7 46.7 %copy.62 = bf16[512,64,4,64]{3,1,2,0:T(8,128)(2,1)} copy(bf16[512,64,4,64]{0,3,2,1:T(8,128)(2,1)} %bitcast.80) | data formatting | bytes 33554432 | tf_op jit(solution)/shard_map/reshape | solution.py:20
  1312.0 24.6 copy.66
  1336.6 46.6 %copy.67 = bf16[512,64,4,64]{3,1,2,0:T(8,128)(2,1)} copy(bf16[512,64,4,64]{0,3,2,1:T(8,128)(2,1)} %bitcast.81) | data formatting | bytes 33554432 | tf_op jit(solution)/shard_map/reshape | solution.py:20
  1428.9 23.7 copy.71
  1452.6 46.7 %copy.72 = bf16[512,64,4,64]{3,1,2,0:T(8,128)(2,1)} copy(bf16[512,64,4,64]{0,3,2,1:T(8,128)(2,1)} %bitcast.82) | data formatting | bytes 33554432 | tf_op jit(solution)/shard_map/reshape | solution.py:20
  1544.9 23.7 copy.76
  1568.6 47.1 %copy.77 = bf16[512,64,4,64]{3,1,2,0:T(8,128)(2,1)} copy(bf16[512,64,4,64]{0,3,2,1:T(8,128)(2,1)} %bitcast.83) | data formatting | bytes 33554432 | tf_op jit(solution)/shard_map/reshape | solution.py:20
  1661.3 24.5 copy.81
  1685.8 46.7 %copy.82 = bf16[512,64,4,64]{3,1,2,0:T(8,128)(2,1)} copy(bf16[512,64,4,64]{0,3,2,1:T(8,128)(2,1)} %bitcast.84) | data formatting | bytes 33554432 | tf_op jit(solution)/shard_map/reshape | solution.py:20
  1732.6 37.3 %fusion.16 = f32[512,64,4,64]{3,1,2,0:T(8,128)} fusion(bf16[512,64,4,64]{3,1,2,0:T(8,128)(2,1)} %copy.62, bf16[512,64,64,1]{2,1,3,0:T(8,128)(2,1)} %copy.86), kind=kOutput, calls=%fused_computation.49 | convolution fusion | flops 1073741824 | bytes 54525952 | tf_op jit(solution)/shard_map/plvr,psr->plvs/dot_general | solution.py:18
  1769.8 37.2 %fusion.17 = f32[512,64,4,64]{3,1,2,0:T(8,128)} fusion(bf16[512,64,4,64]{3,1,2,0:T(8,128)(2,1)} %copy.67, bf16[512,64,64,1]{2,1,3,0:T(8,128)(2,1)} %copy.87), kind=kOutput, calls=%fused_computation.50 | convolution fusion | flops 1073741824 | bytes 54525952 | tf_op jit(solution)/shard_map/plvr,psr->plvs/dot_general | solution.py:18
  1807.1 37.2 %fusion.18 = f32[512,64,4,64]{3,1,2,0:T(8,128)} fusion(bf16[512,64,4,64]{3,1,2,0:T(8,128)(2,1)} %copy.72, bf16[512,64,64,1]{2,1,3,0:T(8,128)(2,1)} %copy.88), kind=kOutput, calls=%fused_computation.51 | convolution fusion | flops 1073741824 | bytes 54525952 | tf_op jit(solution)/shard_map/plvr,psr->plvs/dot_general | solution.py:18
  1844.2 37.4 %fusion.19 = f32[512,64,4,64]{3,1,2,0:T(8,128)} fusion(bf16[512,64,4,64]{3,1,2,0:T(8,128)(2,1)} %copy.77, bf16[512,64,64,1]{2,1,3,0:T(8,128)(2,1)} %copy.89), kind=kOutput, calls=%fused_computation.52 | convolution fusion | flops 1073741824 | bytes 54525952 | tf_op jit(solution)/shard_map/plvr,psr->plvs/dot_general | solution.py:18
  1881.6 104.8 %add_convert_fusion = bf16[512,64,4,64]{3,1,2,0:T(8,128)(2,1)} fusion(f32[512,64,4,64]{3,1,2,0:T(8,128)} %fusion.19, f32[512,64,4,64]{3,1,2,0:T(8,128)} %fusion.18, f32[512,64,4,64]{3,1,2,0:T(8,128)} %fusion.16, f32[512,64,4,64]{3,1,2,0:T(8,128)} %fusion.17, bf16[512,64,4,64]{3,1,2,0:T(8,128)(2,1)} %copy.82, bf16[512,64,64,1]{2,1,3,0:T(8,128)(2,1)} %copy.90), kind=kOutput, calls=%fused_computation.3 | convolution fusion | flops 1115684864 | bytes 171966464 | tf_op jit(solution)/shard_map/plvr,psr->plvs/dot_general | solution.py:18
  1986.4 35.4 %copy.84 = bf16[512,64,4,64]{0,3,2,1:T(8,128)(2,1)} copy(bf16[512,64,4,64]{3,1,2,0:T(8,128)(2,1)} %add_convert_fusion) | data formatting | bytes 33554432 | tf_op jit(solution)/shard_map/convert_element_type | solution.py:24
  2051.2 361.6 %all-to-all-done.2 = bf16[512,64,256]{2,1,0:T(8,128)(2,1)} async-done(((bf16[512,64,256]{2,1,0:T(8,128)(2,1)}), bf16[512,64,256]{2,1,0:T(8,128)(2,1)}, u32[]{:S(2)}, u32[]{:S(2)}) %all-to-all-start.2) | async-done | bytes 16777248 | tf_op jit(solution)/shard_map/all_to_all | solution.py:92
  2427.3 151.6 %all-reduce.2.cloned.1.call-done = bf16[32,8,64,256]{3,2,1,0:T(8,128)(2,1)} async-done(((bf16[32,8,64,256]{3,2,1,0:T(8,128)(2,1)}), bf16[32,8,64,256]{3,2,1,0:T(8,128)(2,1)}) %all-reduce.2.cloned.1.call-update) | async-done | bytes 8388624 | tf_op jit(solution)/shard_map/psum | solution.py:94
  (63 shorter events, 419.7 us)
Async XLA Ops:
  17.6 77.3 %copy-start.1 = (s32[256,1]{0,1:T(1,128)}, s32[256,1]{0,1:T(1,128)S(1)}, u32[]{:S(2)}) copy-start(s32[256,1]{0,1:T(1,128)S(1)} %compare_select_fusion) | copy-start | bytes 3076
  81.4 731.6 %all-to-all-start = ((bf16[512,5,4096]{2,1,0:T(8,128)(2,1)}), bf16[512,5,4096]{2,1,0:T(8,128)(2,1)}, u32[]{:S(2)}, u32[]{:S(2)}) async-start(bf16[512,5,4096]{2,1,0:T(8,128)(2,1)} %scatter_fusion), calls=%async_computation | async-start | bytes 67108864 | tf_op jit(solution)/shard_map/all_to_all | solution.py:89
  132.1 687.6 %copy-start = (bf16[32,5,4096]{2,0,1:T(8,128)(2,1)S(1)}, bf16[32,5,4096]{2,0,1:T(8,128)(2,1)}, u32[]{:S(2)}) copy-start(bf16[32,5,4096]{2,0,1:T(8,128)(2,1)} %param.8) | copy-start | bytes 3932164
  813.0 368.8 %all-to-all-start.1 = ((bf16[512,64,256]{2,1,0:T(8,128)(2,1)}), bf16[512,64,256]{2,1,0:T(8,128)(2,1)}, u32[]{:S(2)}, u32[]{:S(2)}) async-start(bf16[512,64,256]{2,1,0:T(8,128)(2,1)} %scatter_fusion.1), calls=%async_computation.1 | async-start | bytes 33554432 | tf_op jit(solution)/shard_map/all_to_all | solution.py:88
  2045.2 5.9 copy-start.2
  2045.2 367.6 %all-to-all-start.2 = ((bf16[512,64,256]{2,1,0:T(8,128)(2,1)}), bf16[512,64,256]{2,1,0:T(8,128)(2,1)}, u32[]{:S(2)}, u32[]{:S(2)}) async-start(bf16[512,64,256]{2,1,0:T(8,128)(2,1)} %copy.85), calls=%async_computation.2 | async-start | bytes 33554432 | tf_op jit(solution)/shard_map/all_to_all | solution.py:92
  2051.1 527.9 %all-reduce.2.cloned.1.call-start = ((), (), s32[]{:S(2)}) async-start(), calls=%async_computation.3 | async-start | bytes 16777216 | tf_op jit(solution)/shard_map/psum | solution.py:94
Sparse Core Ops, SparseCore 0:
  2427.5 151.4 all-reduce.1
where the time goes:
time: 2610 us; the launch traced here: 2590 us
  waiting for transfers between devices  1310 us (50%)
  local copies, waits for them, and re-layouts  898 us (34%)
  matrix products  336 us (13%)
    all_to_all x1, waiting for transfers between devices, per_device(): lax.all_to_all(send_left, 'bond', split_axis=0, concat_axis=0, tiled=True)  681 us
    all_to_all x1, waiting for transfers between devices, per_device(): lax.all_to_all(partial_sum, 'bond', split_axis=0, concat_axis=0, tiled=True)  362 us
    dot_general x5, matrix products, apply_terms(): jnp.einsum('plvr,psr->plvs', sectioned.reshape(slot_count, block_width, v...  254 us
    reshape x5, local copies, waits for them, and re-layouts, apply_terms(): sectioned.reshape(slot_count, block_width, vectors, block_width)  234 us
    slice x6, local copies, waits for them, and re-layouts, apply_terms(): left_term = left_rows[:, term].reshape(slot_count, block_width, block_width)  184 us
    psum x1, waiting for transfers between devices, per_device(): summed = lax.psum(returned.astype(jnp.float32).astype(jnp.bfloat16), 'mpo')  152 us
    convert_element_type x5, local copies, waits for them, and re-layouts, apply_terms(): sectioned = jnp.einsum('plk,pkc->plc', left_term, wave_rows, preferred_el...  120 us
    all_to_all x1, waiting for transfers between devices, per_device(): lax.all_to_all(send_wave, 'bond', split_axis=0, concat_axis=0, tiled=True)  120 us
  transfers between devices with their start and end apart: 4, of which 4 were waited for; matrix products, arithmetic and copies ran while one was open for 11% of the time, Pallas kernels for 0%

commit v1 on v0

v1 whole, which is shorter than its diff:
```python
import functools

import jax
import jax.numpy as jnp
from jax import lax
from jax.experimental import pallas as pl
from jax.experimental.pallas import tpu as pltpu
from jax.sharding import PartitionSpec as P


def pack_right(right_env, width):
    sectors, terms, _ = right_env.shape
    turned = jnp.swapaxes(right_env.reshape(sectors, terms, width, width), 2, 3)
    pairs = terms // 2
    parts = []
    if pairs:
        even = turned[:, : 2 * pairs].reshape(sectors, pairs, 2, width, width)
        even = jnp.swapaxes(even, 2, 3).reshape(sectors, pairs * width, 2 * width)
        parts.append(even)
    if terms % 2:
        odd = turned[:, -1].reshape(sectors, 2, width // 2, width)
        parts.append(jnp.swapaxes(odd, 1, 2).reshape(sectors, width // 2, 2 * width))
    return jnp.concatenate(parts, axis=1) if len(parts) > 1 else parts[0]


def block_result(wave, left_scaled, packed, terms, width):
    lanes = 2 * width
    lane = lax.broadcasted_iota(jnp.int32, (1, lanes), 1)
    low = (lane < width).astype(jnp.bfloat16)
    high = (lane >= width).astype(jnp.bfloat16)
    rolled = jnp.concatenate([packed[:, width:], packed[:, :width]], axis=1)
    groups = wave.shape[1] // lanes
    rows = jnp.concatenate([wave[:, g * lanes : (g + 1) * lanes] for g in range(groups)], axis=0)
    spread = []
    for pair in range(terms // 2):
        here, there = (m[pair * width : (pair + 1) * width] for m in (packed, rolled))
        spread.append(jnp.concatenate([here * low, there * high], axis=0))
        spread.append(jnp.concatenate([there * low, here * high], axis=0))
    if terms % 2:
        first = terms // 2 * width
        here, there = (m[first : first + width // 2] for m in (packed, rolled))
        spread.append(jnp.concatenate([here * low, there * low, there * high, here * high], axis=0))
    stacked = []
    for first in range(0, terms, 2):
        both = jnp.concatenate(spread[first : first + 2], axis=1)
        product = jnp.dot(rows, both, preferred_element_type=jnp.float32).astype(jnp.bfloat16)
        for term in range(both.shape[1] // lanes):
            cut = product[:, term * lanes : (term + 1) * lanes]
            stacked.append(
                jnp.concatenate([cut[g * width : (g + 1) * width] for g in range(groups)], axis=1)
            )
    stacked = jnp.concatenate(stacked, axis=0)
    return jnp.dot(left_scaled, stacked, preferred_element_type=jnp.float32)


def contract_kernel(terms, width, sector_ref, wave_ref, left_ref, gain_ref, right_ref, out_ref):
    classes = wave_ref.shape[1]
    row = pl.program_id(0)
    left = left_ref[0].astype(jnp.float32)
    for charge in range(classes):
        sector = sector_ref[row * classes + charge]
        left_scaled = (left * gain_ref[charge : charge + 1, :]).astype(jnp.bfloat16)
        out_ref[0, charge] = block_result(
            wave_ref[0, charge], left_scaled, right_ref[sector], terms, width
        ).astype(out_ref.dtype)


def per_device(wave_blocks, left_env, right_env, mpo_coef, mpo_mask, right_sector):
    sec_local, classes, width, columns = wave_blocks.shape
    terms = left_env.shape[1]
    bond_index = lax.axis_index("bond")
    gains = jnp.repeat((mpo_coef * mpo_mask.astype(jnp.float32)).T, width, axis=1)
    packed = pack_right(right_env, width)
    gathered = lax.all_gather(packed, "bond", axis=0, tiled=True)
    left_rows = jnp.swapaxes(left_env.reshape(sec_local, terms, width, width), 1, 2)
    left_rows = left_rows.reshape(sec_local, width, terms * width)
    sectors = lax.dynamic_slice_in_dim(right_sector, bond_index * sec_local, sec_local, 0)
    partial = pl.pallas_call(
        functools.partial(contract_kernel, terms, width),
        out_shape=jax.ShapeDtypeStruct(wave_blocks.shape, jnp.bfloat16),
        grid_spec=pltpu.PrefetchScalarGridSpec(
            num_scalar_prefetch=1,
            grid=(sec_local,),
            in_specs=[
                pl.BlockSpec((1, classes, width, columns), lambda i, s: (i, 0, 0, 0)),
                pl.BlockSpec((1, width, terms * width), lambda i, s: (i, 0, 0)),
                pl.BlockSpec(gains.shape, lambda i, s: (0, 0)),
                pl.BlockSpec(gathered.shape, lambda i, s: (0, 0, 0)),
            ],
            out_specs=pl.BlockSpec((1, classes, width, columns), lambda i, s: (i, 0, 0, 0)),
        ),
        compiler_params=pltpu.CompilerParams(vmem_limit_bytes=48 << 20),
    )(sectors.reshape(-1), wave_blocks, left_rows, gains, gathered)
    return lax.psum(partial, "mpo")


def solution(mesh):
    return jax.shard_map(
        per_device,
        mesh=mesh,
        in_specs=(
            P("bond", None, None, None),
            P("bond", "mpo", None),
            P("bond", "mpo", None),
            P("mpo", None),
            P("mpo", None),
            P(),
        ),
        out_specs=P("bond", None, None, None),
        check_vma=False,
    )
```

time: 2610 us -> 398 us (0.15)
  waiting for transfers between devices: 1310 us -> 294 us
  local copies, waits for them, and re-layouts: 898 us -> 33 us
  matrix products: 336 us -> 0 us
  Pallas kernels: 0 us -> 55.4 us
    all_to_all x3 -> x0, waiting for transfers between devices: 1160 us -> none  [the longest x1 681 us: per_device(): lax.all_to_all(send_left, 'bond', split_axis=0, concat_axis=0, tiled=True)]
    dot_general x12 -> x0, matrix products: 336 us -> none  [the longest x5 254 us: apply_terms(): jnp.einsum('plvr,psr->plvs', sectioned.reshape(slot_count, block_width, v...]
    reshape x8, local copies, waits for them, and re-layouts: 234 us -> 15.4 us  [the longest x2 6.39 us: per_device(): left_env.reshape(sec_local, terms, width, width)]
    convert_element_type x11 -> x0, local copies, waits for them, and re-layouts: 211 us -> none  [the longest x5 120 us: apply_terms(): sectioned = jnp.einsum('plk,pkc->plc', left_term, wave_rows, preferred_el...]
    slice x9 -> x3, local copies, waits for them, and re-layouts: 199 us -> 3.63 us  [the longest x2 2.14 us: pack_right(): odd = turned[:, -1].reshape(sectors, 2, width // 2, width)]
    all_gather x0 -> x1, waiting for transfers between devices: none -> 143 us  [per_device(): gathered = lax.all_gather(packed, 'bond', axis=0, tiled=True)]
    another operation x12 -> x0, local copies, waits for them, and re-layouts: 130 us -> none  [the longest x5 64.8 us: apply_terms(): right_rows[:, term].reshape(slot_count, block_width, block_width)]
    scatter x2 -> x0, local copies, waits for them, and re-layouts: 82.4 us -> none  [the longest x1 45.2 us: per_device(): send_left = jnp.zeros((slot_total, term_local, block_width * block_width)...]
  transfers between devices with their start and end apart: 4 -> 2, of which waited for: 4 -> 2; matrix products, arithmetic and copies ran while one was open for 11% -> 3% of each run, Pallas kernels for 0% -> 0%
where the time goes in v1:
time: 398 us; the launch traced here: 397 us
  waiting for transfers between devices  294 us (74%)
  Pallas kernels  55.4 us (14%)
  local copies, waits for them, and re-layouts  33 us (8%)
  between operations  13.5 us (3%)
    psum x1, waiting for transfers between devices, per_device(): return lax.psum(partial, 'mpo')  151 us
    all_gather x1, waiting for transfers between devices, per_device(): gathered = lax.all_gather(packed, 'bond', axis=0, tiled=True)  143 us
    pallas_call x1, Pallas kernels, per_device(): pl.pallas_call(functools.partial(contract_kernel, terms, width), out_shap...  55.4 us
    unnamed x7, local copies, waits for them, and re-layouts  8.46 us
  transfers between devices with their start and end apart: 2, of which 2 were waited for; matrix products, arithmetic and copies ran while one was open for 3% of the time, Pallas kernels for 0%

profile of v1, /device:TPU:0, one launch (start us, length us, event | category | flops | bytes accessed | tf_op | source)
XLA Modules:
  0.0 397.5 jit_solution(4852777657983779471)
XLA Ops:
  6.5 3.8 reshape.28
  10.4 0.8 slice.9
  11.2 1.5 slice.8
  12.7 4.8 %copy.33 = bf16[32,2,64,2,64]{4,3,2,1,0:T(2,128)(2,1)S(1)} copy(bf16[32,2,64,2,64]{2,4,0,3,1:T(8,128)(2,1)} %bitcast.19) | data formatting | bytes 2097152 | tf_op jit(solution)/shard_map/transpose | solution.py:18
  17.5 1.0 reshape.30
  18.5 1.3 copy.34
  19.8 0.5 copy.35
  20.4 0.3 reshape.31
  20.6 1.2 pad_maximum_fusion
  21.8 0.0 all-reduce.2.cloned.1.call-start
  21.9 0.1 copy.31
  22.0 0.1 constant_dynamic-slice_fusion
  22.1 0.1 copy.29
  22.1 0.1 reshape.24.sector_ref
  22.2 0.1 broadcast_in_dim.3
  22.3 0.1 reshape.27.gain_ref
  22.4 3.8 reshape.25
  26.2 2.6 copy.30
  28.8 3.7 copy.36.left_ref
  32.5 143.1 %all-gather.2.cloned.1.call-done.right_ref = bf16[256,160,128]{2,1,0:T(8,128)(2,1)} async-done(((bf16[32,160,128]{2,1,0:T(8,128)(2,1)}), bf16[256,160,128]{2,1,0:T(8,128)(2,1)}) %all-gather.2.cloned.1.call-update) | async-done | bytes 10485776 | tf_op jit(solution)/shard_map/all_gather | solution.py:74
  175.5 55.4 %shard_map.64 = bf16[32,8,64,256]{3,2,1,0:T(8,128)(2,1)} custom-call(s32[256]{0:T(256)S(1)} %reshape.24.sector_ref, bf16[32,8,64,256]{3,2,1,0:T(8,128)(2,1)} %wave_ref.1, bf16[32,64,320]{2,1,0:T(8,128)(2,1)S(1)} %copy.36.left_ref, f32[8,320]{1,0:T(8,128)S(1)} %reshape.27.gain_ref, bf16[256,160,128]{2,1,0:T(8,128)(2,1)} %all-gather.2.cloned.1.call-done.right_ref), custom_call_target="tpu_custom_call" | custom-call | tf_op jit(solution)/shard_map/pallas_call | solution.py:78
  231.0 0.0 all-reduce.2.cloned.1.call-update
  231.0 151.2 %all-reduce.2.cloned.1.call-done = bf16[32,8,64,256]{3,2,1,0:T(8,128)(2,1)} async-done(((bf16[32,8,64,256]{3,2,1,0:T(8,128)(2,1)}), bf16[32,8,64,256]{3,2,1,0:T(8,128)(2,1)}) %all-reduce.2.cloned.1.call-update) | async-done | bytes 8388624 | tf_op jit(solution)/shard_map/psum | solution.py:94
  382.2 8.4 %copy.39 = bf16[32,8,64,256]{3,2,1,0:T(8,128)(2,1)} copy(bf16[32,8,64,256]{3,2,1,0:T(8,128)(2,1)} %all-reduce.2.cloned.1.call-done) | data formatting | bytes 16777216
  (9 shorter events, 0.0 us)
Async XLA Ops:
  6.5 15.5 %copy-start = (s32[256,8]{0,1:T(8,128)S(1)}, s32[256,8]{0,1:T(8,128)}, u32[]{:S(2)}) copy-start(s32[256,8]{0,1:T(8,128)} %param.11) | copy-start | bytes 24580
  6.5 169.0 %all-gather.2.cloned.1.call-start = ((), (), s32[]{:S(2)}) async-start(), calls=%async_computation | async-start | bytes 11796480 | tf_op jit(solution)/shard_map/all_gather | solution.py:74
  20.3 1.5 copy-start.1
  20.4 1.5 copy-start.2
  21.8 360.4 %all-reduce.2.cloned.1.call-start = ((), (), s32[]{:S(2)}) async-start(), calls=%async_computation.1 | async-start | bytes 16777216 | tf_op jit(solution)/shard_map/psum | solution.py:94
Sparse Core Ops, SparseCore 0:
  21.9 153.5 all-gather.1
  231.1 151.0 all-reduce.1

commit v2 on v1

--- a/solution.py
+++ b/solution.py
@@ -53,16 +53,105 @@
     return jnp.dot(left_scaled, stacked, preferred_element_type=jnp.float32)
 
 
-def contract_kernel(terms, width, sector_ref, wave_ref, left_ref, gain_ref, right_ref, out_ref):
-    classes = wave_ref.shape[1]
-    row = pl.program_id(0)
-    left = left_ref[0].astype(jnp.float32)
-    for charge in range(classes):
-        sector = sector_ref[row * classes + charge]
-        left_scaled = (left * gain_ref[charge : charge + 1, :]).astype(jnp.bfloat16)
-        out_ref[0, charge] = block_result(
-            wave_ref[0, charge], left_scaled, right_ref[sector], terms, width
-        ).astype(out_ref.dtype)
+MESH = pl.DeviceIdType.MESH
+LAG = 2
+
+
+def contract_kernel(
+    terms, width, sector_ref, wave_ref, left_ref, gain_ref, right_ref, out_ref,
+    mine, theirs, pair_in, pair_sum, far_in, sent, got,
+):
+    sectors, classes = wave_ref.shape[:2]
+    steps = sectors // 2
+    place = lax.axis_index("mpo")
+    side = lax.rem(place, 2)
+    pair = place + 1 - 2 * side
+    far = lax.rem(place + 2, 4)
+
+    barrier = pltpu.get_barrier_semaphore()
+    for other in (pair, far):
+        pl.semaphore_signal(barrier, inc=1, device_id={"mpo": other}, device_id_type=MESH)
+    pl.semaphore_wait(barrier, 2)
+
+    def send(kind, step, source, target, other):
+        return pltpu.make_async_remote_copy(
+            src_ref=source,
+            dst_ref=target,
+            send_sem=sent.at[kind, step],
+            recv_sem=got.at[kind, step],
+            device_id={"mpo": other},
+            device_id_type=MESH,
+        )
+
+    def to_pair(step):
+        return send(0, step, theirs.at[step], pair_in.at[step], pair)
+
+    def to_far(step):
+        return send(1, step, pair_sum.at[step], far_in.at[step], far)
+
+    def total_copy(step, row):
+        return send(2, step, out_ref.at[row], out_ref.at[row], pair)
+
+    def contract(row, store):
+        left = left_ref[row].astype(jnp.float32)
+        unroll = 4 if classes % 4 == 0 else 1
+
+        @pl.loop(0, classes // unroll)
+        def _(outer):
+            for inner in range(unroll):
+                charge = outer * unroll + inner
+                sector = sector_ref[row * classes + charge]
+                left_scaled = (left * gain_ref[charge]).astype(jnp.bfloat16)
+                store(
+                    charge,
+                    block_result(wave_ref[row, charge], left_scaled, right_ref[sector], terms, width),
+                )
+
+    def finish(step):
+        to_far(step).wait_recv()
+        row = 2 * step + side
+
+        @pl.loop(0, classes)
+        def _(charge):
+            total = pair_sum[step, charge].astype(jnp.float32) + far_in[step, charge].astype(jnp.float32)
+            out_ref[row, charge] = total.astype(out_ref.dtype)
+
+        total_copy(step, row).start()
+
+    @pl.loop(0, steps)
+    def _(step):
+        def store_theirs(charge, value):
+            theirs[step, charge] = value.astype(jnp.bfloat16)
+
+        def store_mine(charge, value):
+            mine[charge] = value
+
+        contract(2 * step + 1 - side, store_theirs)
+        to_pair(step).start()
+        contract(2 * step + side, store_mine)
+        to_pair(step).wait_recv()
+
+        @pl.loop(0, classes)
+        def _(charge):
+            both = mine[charge] + pair_in[step, charge].astype(jnp.float32)
+            pair_sum[step, charge] = both.astype(jnp.bfloat16)
+
+        to_far(step).start()
+
+        @pl.when(step >= LAG)
+        def _():
+            finish(step - LAG)
+
+    @pl.loop(max(0, steps - LAG), steps)
+    def _(step):
+        finish(step)
+
+    @pl.loop(0, steps)
+    def _(step):
+        to_pair(step).wait_send()
+        to_far(step).wait_send()
+        total_copy(step, 2 * step + side).wait_send()
+        total_copy(step, 2 * step + 1 - side).wait_recv()
 
 
 def per_device(wave_blocks, left_env, right_env, mpo_coef, mpo_mask, right_sector):
@@ -75,23 +164,27 @@
     left_rows = jnp.swapaxes(left_env.reshape(sec_local, terms, width, width), 1, 2)
     left_rows = left_rows.reshape(sec_local, width, terms * width)
     sectors = lax.dynamic_slice_in_dim(right_sector, bond_index * sec_local, sec_local, 0)
-    partial = pl.pallas_call(
+    steps = sec_local // 2
+    slots = pltpu.VMEM((steps, classes, width, columns), jnp.bfloat16)
+    vmem = pl.BlockSpec(memory_space=pltpu.VMEM)
+    return pl.pallas_call(
         functools.partial(contract_kernel, terms, width),
         out_shape=jax.ShapeDtypeStruct(wave_blocks.shape, jnp.bfloat16),
-        grid_spec=pltpu.PrefetchScalarGridSpec(
-            num_scalar_prefetch=1,
-            grid=(sec_local,),
-            in_specs=[
-                pl.BlockSpec((1, classes, width, columns), lambda i, s: (i, 0, 0, 0)),
-                pl.BlockSpec((1, width, terms * width), lambda i, s: (i, 0, 0)),
-                pl.BlockSpec(gains.shape, lambda i, s: (0, 0)),
-                pl.BlockSpec(gathered.shape, lambda i, s: (0, 0, 0)),
-            ],
-            out_specs=pl.BlockSpec((1, classes, width, columns), lambda i, s: (i, 0, 0, 0)),
+        in_specs=[pl.BlockSpec(memory_space=pltpu.SMEM), vmem, vmem, vmem, vmem],
+        out_specs=vmem,
+        scratch_shapes=[
+            pltpu.VMEM((classes, width, columns), jnp.float32),
+            slots,
+            slots,
+            slots,
+            slots,
+            pltpu.SemaphoreType.DMA((3, steps)),
+            pltpu.SemaphoreType.DMA((3, steps)),
+        ],
+        compiler_params=pltpu.CompilerParams(
+            collective_id=0, has_side_effects=True, vmem_limit_bytes=56 << 20
         ),
-        compiler_params=pltpu.CompilerParams(vmem_limit_bytes=48 << 20),
-    )(sectors.reshape(-1), wave_blocks, left_rows, gains, gathered)
-    return lax.psum(partial, "mpo")
+    )(sectors.reshape(-1), wave_blocks, left_rows, gains[:, None, :], gathered)
 
 
 def solution(mesh):

time: 398 us -> 300 us (0.75)
  waiting for transfers between devices: 294 us -> 142 us
  Pallas kernels: 55.4 us -> 109 us
    psum x1 -> x0, waiting for transfers between devices: 151 us -> none  [per_device(): return lax.psum(partial, 'mpo')]
    pallas_call x1, Pallas kernels: 55.4 us -> 109 us  [per_device(): pl.pallas_call(functools.partial(contract_kernel, terms, width), out_shap...]
    unnamed x7 -> x9, local copies, waits for them, and re-layouts: 8.46 us -> 8.46 us
  transfers between devices with their start and end apart: 2 -> 1, of which waited for: 2 -> 1; matrix products, arithmetic and copies ran while one was open for 3% -> 4% of each run, Pallas kernels for 0% -> 0%
where the time goes in v2:
time: 300 us
  waiting for transfers between devices  142 us (47%)
  Pallas kernels  109 us (36%)
  local copies, waits for them, and re-layouts  33.9 us (11%)
  between operations  13.5 us (4%)
    all_gather x1, waiting for transfers between devices, per_device(): gathered = lax.all_gather(packed, 'bond', axis=0, tiled=True)  142 us
    pallas_call x1, Pallas kernels, per_device(): pl.pallas_call(functools.partial(contract_kernel, terms, width), out_shap...  109 us
    unnamed x9, local copies, waits for them, and re-layouts  8.46 us
    reshape x2, local copies, waits for them, and re-layouts, per_device(): left_env.reshape(sec_local, terms, width, width)  7.08 us
  transfers between devices with their start and end apart: 1, of which 1 were waited for; matrix products, arithmetic and copies ran while one was open for 4% of the time, Pallas kernels for 0%

profile of v2, /device:TPU:0, one launch (start us, length us, event | category | flops | bytes accessed | tf_op | source)
XLA Modules:
  0.0 299.7 jit_solution(14238769979983606308)
XLA Ops:
  6.5 3.8 %reshape.24 = bf16[32,5,64,64]{3,2,0,1:T(8,128)(2,1)S(1)} reshape(bf16[32,5,4096]{2,0,1:T(8,128)(2,1)} %param.8) | data formatting | bytes 2621440 | tf_op jit(solution)/shard_map/reshape | solution.py:13
  10.4 0.8 slice.9
  11.2 1.5 slice.8
  12.7 4.8 %copy.36 = bf16[32,2,64,2,64]{4,3,2,1,0:T(2,128)(2,1)S(1)} copy(bf16[32,2,64,2,64]{2,4,0,3,1:T(8,128)(2,1)} %bitcast.19) | data formatting | bytes 2097152 | tf_op jit(solution)/shard_map/transpose | solution.py:18
  17.5 1.0 reshape.26
  18.5 1.3 copy.37
  19.8 0.5 copy.38
  20.3 0.0 copy-start.2
  20.4 0.0 copy-start.3
  20.4 0.3 reshape.27
  20.7 1.2 pad_maximum_fusion
  21.8 0.0 all-gather.2.cloned.1.call-update
  21.9 0.1 copy.34
  22.0 0.1 constant_dynamic-slice_fusion
  22.0 0.1 copy.32
  22.1 0.7 reshape.21.sector_ref
  22.8 0.1 broadcast_in_dim.3
  22.9 0.7 broadcast_in_dim_reshape.4.gain_ref
  23.5 3.9 %reshape.22 = bf16[32,5,64,64]{3,2,0,1:T(8,128)(2,1)} reshape(bf16[32,5,4096]{2,0,1:T(8,128)(2,1)S(1)} %copy-done.1) | data formatting | bytes 2621440 | tf_op jit(solution)/shard_map/reshape | solution.py:164
  27.4 3.2 %copy.33 = bf16[32,5,64,64]{2,3,1,0:T(8,128)(2,1)S(1)} copy(bf16[32,5,64,64]{3,2,0,1:T(8,128)(2,1)} %reshape.22) | data formatting | bytes 2621440 | tf_op jit(solution)/shard_map/reshape | solution.py:164
  30.6 2.7 copy.39.left_ref
  33.3 142.2 %all-gather.2.cloned.1.call-done.right_ref = bf16[256,160,128]{2,1,0:T(8,128)(2,1)} async-done(((bf16[32,160,128]{2,1,0:T(8,128)(2,1)}), bf16[256,160,128]{2,1,0:T(8,128)(2,1)}) %all-gather.2.cloned.1.call-update) | async-done | bytes 10485776 | tf_op jit(solution)/shard_map/all_gather | solution.py:163
  175.5 108.9 %shard_map.64 = bf16[32,8,64,256]{3,2,1,0:T(8,128)(2,1)} custom-call(s32[256]{0:T(256)} %reshape.21.sector_ref, bf16[32,8,64,256]{3,2,1,0:T(8,128)(2,1)} %wave_ref.1, bf16[32,64,320]{2,1,0:T(8,128)(2,1)} %copy.39.left_ref, f32[8,1,320]{2,1,0:T(1,128)} %broadcast_in_dim_reshape.4.gain_ref, bf16[256,160,128]{2,1,0:T(8,128)(2,1)} %all-gather.2.cloned.1.call-done.right_ref), custom_call_target="tpu_custom_call" | custom-call | tf_op jit(solution)/shard_map/pallas_call | solution.py:170
  284.5 8.4 %copy.43 = bf16[32,8,64,256]{3,2,1,0:T(8,128)(2,1)} copy(bf16[32,8,64,256]{3,2,1,0:T(8,128)(2,1)} %shard_map.64) | data formatting | bytes 16777216
  (8 shorter events, 0.0 us)
Async XLA Ops:
  6.5 15.4 %copy-start = (s32[256,8]{0,1:T(8,128)S(1)}, s32[256,8]{0,1:T(8,128)}, u32[]{:S(2)}) copy-start(s32[256,8]{0,1:T(8,128)} %param.11) | copy-start | bytes 24580
  6.5 169.0 %all-gather.2.cloned.1.call-start = ((), (), s32[]{:S(2)}) async-start(), calls=%async_computation | async-start | bytes 11796480 | tf_op jit(solution)/shard_map/all_gather | solution.py:163
  20.3 1.5 copy-start.2
  20.4 1.5 copy-start.3
  20.4 3.2 %copy-start.1 = (bf16[32,5,4096]{2,0,1:T(8,128)(2,1)S(1)}, bf16[32,5,4096]{2,0,1:T(8,128)(2,1)}, u32[]{:S(2)}) copy-start(bf16[32,5,4096]{2,0,1:T(8,128)(2,1)} %param.7) | copy-start | bytes 3932164
Sparse Core Ops, SparseCore 0:
  22.0 153.5 all-gather.1

commit v3 on v2

--- a/solution.py
+++ b/solution.py
@@ -10,15 +10,15 @@
 
 def pack_right(right_env, width):
     sectors, terms, _ = right_env.shape
-    turned = jnp.swapaxes(right_env.reshape(sectors, terms, width, width), 2, 3)
+    squares = right_env.reshape(sectors, terms, width, width)
     pairs = terms // 2
     parts = []
     if pairs:
-        even = turned[:, : 2 * pairs].reshape(sectors, pairs, 2, width, width)
+        even = squares[:, : 2 * pairs].reshape(sectors, pairs, 2, width, width)
         even = jnp.swapaxes(even, 2, 3).reshape(sectors, pairs * width, 2 * width)
         parts.append(even)
     if terms % 2:
-        odd = turned[:, -1].reshape(sectors, 2, width // 2, width)
+        odd = squares[:, -1].reshape(sectors, 2, width // 2, width)
         parts.append(jnp.swapaxes(odd, 1, 2).reshape(sectors, width // 2, 2 * width))
     return jnp.concatenate(parts, axis=1) if len(parts) > 1 else parts[0]
 
@@ -42,9 +42,11 @@
         spread.append(jnp.concatenate([here * low, there * low, there * high, here * high], axis=0))
     stacked = []
     for first in range(0, terms, 2):
-        both = jnp.concatenate(spread[first : first + 2], axis=1)
-        product = jnp.dot(rows, both, preferred_element_type=jnp.float32).astype(jnp.bfloat16)
-        for term in range(both.shape[1] // lanes):
+        both = jnp.concatenate(spread[first : first + 2], axis=0)
+        product = lax.dot_general(
+            rows, both, (((1,), (1,)), ((), ())), preferred_element_type=jnp.float32
+        ).astype(jnp.bfloat16)
+        for term in range(both.shape[0] // lanes):
             cut = product[:, term * lanes : (term + 1) * lanes]
             stacked.append(
                 jnp.concatenate([cut[g * width : (g + 1) * width] for g in range(groups)], axis=1)

time: 300 us -> 300 us (level)
    slice x3, local copies, waits for them, and re-layouts: 3.63 us -> 0.18 us  [the longest x1 0.17 us: pack_right(): even = squares[:, :2 * pairs].reshape(sectors, pairs, 2, width, width)]
    unnamed x9 -> x11, local copies, waits for them, and re-layouts: 8.46 us -> 9.77 us
where the time goes in v3:
time: 300 us
  waiting for transfers between devices  142 us (47%)
  Pallas kernels  109 us (36%)
  local copies, waits for them, and re-layouts  33.4 us (11%)
  between operations  13.5 us (4%)
    all_gather x1, waiting for transfers between devices, per_device(): gathered = lax.all_gather(packed, 'bond', axis=0, tiled=True)  142 us
    pallas_call x1, Pallas kernels, per_device(): pl.pallas_call(functools.partial(contract_kernel, terms, width), out_shap...  109 us
    unnamed x11, local copies, waits for them, and re-layouts  9.77 us
    reshape x2, local copies, waits for them, and re-layouts, per_device(): left_env.reshape(sec_local, terms, width, width)  7.08 us
  transfers between devices with their start and end apart: 1, of which 1 were waited for; matrix products, arithmetic and copies ran while one was open for 4% of the time, Pallas kernels for 0%

profile of v3, /device:TPU:0, one launch (start us, length us, event | category | flops | bytes accessed | tf_op | source)
XLA Modules:
  0.0 299.6 jit_solution(3962081119847262661)
XLA Ops:
  6.5 3.8 %reshape.24 = bf16[32,5,64,64]{3,2,0,1:T(8,128)(2,1)S(1)} reshape(bf16[32,5,4096]{2,0,1:T(8,128)(2,1)} %param.8) | data formatting | bytes 2621440 | tf_op jit(solution)/shard_map/reshape | solution.py:13
  10.4 0.0 copy-start.1
  10.4 0.2 slice.8
  10.6 1.3 copy-done.1
  11.9 3.5 %copy.35 = bf16[32,2,64,2,64]{4,3,2,1,0:T(2,128)(2,1)} copy(bf16[32,2,64,2,64]{4,2,0,3,1:T(8,128)(2,1)S(1)} %bitcast.17) | data formatting | bytes 2097152 | tf_op jit(solution)/shard_map/transpose | solution.py:18
  15.4 3.9 %reshape.26 = bf16[32,128,128]{2,1,0:T(8,128)(2,1)S(1)} reshape(bf16[32,2,64,2,64]{4,3,2,1,0:T(2,128)(2,1)} %copy.35) | data formatting | bytes 2097152 | tf_op jit(solution)/shard_map/reshape | solution.py:18
  19.3 0.5 copy.36
  19.9 0.0 copy-start.4
  19.9 0.0 copy-start.2
  19.9 0.3 reshape.27
  20.2 1.2 pad_maximum_fusion
  21.3 0.0 all-gather.2.cloned.1.call-update
  21.4 0.1 copy.33
  21.5 0.1 constant_dynamic-slice_fusion
  21.6 0.1 copy.31
  21.6 0.7 reshape.21.sector_ref
  22.3 0.1 broadcast_in_dim.3
  22.4 0.7 broadcast_in_dim_reshape.4.gain_ref
  23.1 3.9 %reshape.22 = bf16[32,5,64,64]{3,2,0,1:T(8,128)(2,1)} reshape(bf16[32,5,4096]{2,0,1:T(8,128)(2,1)S(1)} %copy-done.2) | data formatting | bytes 2621440 | tf_op jit(solution)/shard_map/reshape | solution.py:166
  26.9 3.2 %copy.32 = bf16[32,5,64,64]{2,3,1,0:T(8,128)(2,1)S(1)} copy(bf16[32,5,64,64]{3,2,0,1:T(8,128)(2,1)} %reshape.22) | data formatting | bytes 2621440 | tf_op jit(solution)/shard_map/reshape | solution.py:166
  30.2 2.7 copy.37.left_ref
  32.9 142.2 %all-gather.2.cloned.1.call-done.right_ref = bf16[256,160,128]{2,1,0:T(8,128)(2,1)} async-done(((bf16[32,160,128]{2,1,0:T(8,128)(2,1)}), bf16[256,160,128]{2,1,0:T(8,128)(2,1)}) %all-gather.2.cloned.1.call-update) | async-done | bytes 10485776 | tf_op jit(solution)/shard_map/all_gather | solution.py:165
  175.1 109.3 %shard_map.64 = bf16[32,8,64,256]{3,2,1,0:T(8,128)(2,1)} custom-call(s32[256]{0:T(256)} %reshape.21.sector_ref, bf16[32,8,64,256]{3,2,1,0:T(8,128)(2,1)} %wave_ref.1, bf16[32,64,320]{2,1,0:T(8,128)(2,1)} %copy.37.left_ref, f32[8,1,320]{2,1,0:T(1,128)} %broadcast_in_dim_reshape.4.gain_ref, bf16[256,160,128]{2,1,0:T(8,128)(2,1)} %all-gather.2.cloned.1.call-done.right_ref), custom_call_target="tpu_custom_call" | custom-call | tf_op jit(solution)/shard_map/pallas_call | solution.py:172
  284.3 8.4 %copy.41 = bf16[32,8,64,256]{3,2,1,0:T(8,128)(2,1)} copy(bf16[32,8,64,256]{3,2,1,0:T(8,128)(2,1)} %shard_map.64) | data formatting | bytes 16777216
  (10 shorter events, 0.0 us)
Async XLA Ops:
  6.5 15.0 %copy-start = (s32[256,8]{0,1:T(8,128)S(1)}, s32[256,8]{0,1:T(8,128)}, u32[]{:S(2)}) copy-start(s32[256,8]{0,1:T(8,128)} %param.11) | copy-start | bytes 24580
  6.5 168.5 %all-gather.2.cloned.1.call-start = ((), (), s32[]{:S(2)}) async-start(), calls=%async_computation | async-start | bytes 11796480 | tf_op jit(solution)/shard_map/all_gather | solution.py:165
  10.4 1.5 copy-start.1
  15.4 4.0 %slice-start = ((bf16[32,5,64,64]{3,2,0,1:T(8,128)(2,1)}), bf16[32,1,64,64]{3,2,0,1:T(8,128)(2,1)S(1)}, s32[]{:S(2)}) async-start(bf16[32,5,64,64]{3,2,0,1:T(8,128)(2,1)} %copy-done.1), calls=%async_computation.1 | async-start | bytes 1048576 | tf_op jit(solution)/shard_map/slice | solution.py:21
  19.9 1.5 copy-start.3
  19.9 1.5 copy-start.4
  19.9 3.2 %copy-start.2 = (bf16[32,5,4096]{2,0,1:T(8,128)(2,1)S(1)}, bf16[32,5,4096]{2,0,1:T(8,128)(2,1)}, u32[]{:S(2)}) copy-start(bf16[32,5,4096]{2,0,1:T(8,128)(2,1)} %param.7) | copy-start | bytes 3932164
Sparse Core Ops, SparseCore 0:
  21.5 153.5 all-gather.1

commit v4 on v3

--- a/solution.py
+++ b/solution.py
@@ -60,8 +60,8 @@
 
 
 def contract_kernel(
-    terms, width, sector_ref, wave_ref, left_ref, gain_ref, right_ref, out_ref,
-    mine, theirs, pair_in, pair_sum, far_in, sent, got,
+    terms, width, sector_ref, wave_hbm, left_ref, gain_ref, right_ref, out_ref,
+    wave_ref, mine, theirs, pair_in, pair_sum, far_in, loaded, sent, got,
 ):
     sectors, classes = wave_ref.shape[:2]
     steps = sectors // 2
@@ -69,6 +69,14 @@
     side = lax.rem(place, 2)
     pair = place + 1 - 2 * side
     far = lax.rem(place + 2, 4)
+
+    def load(step):
+        rows = pl.ds(2 * step, 2)
+        return pltpu.make_async_copy(wave_hbm.at[rows], wave_ref.at[rows], loaded.at[step])
+
+    @pl.loop(0, steps)
+    def _(step):
+        load(step).start()
 
     barrier = pltpu.get_barrier_semaphore()
     for other in (pair, far):
@@ -128,6 +136,7 @@
         def store_mine(charge, value):
             mine[charge] = value
 
+        load(step).wait()
         contract(2 * step + 1 - side, store_theirs)
         to_pair(step).start()
         contract(2 * step + side, store_mine)
@@ -172,14 +181,16 @@
     return pl.pallas_call(
         functools.partial(contract_kernel, terms, width),
         out_shape=jax.ShapeDtypeStruct(wave_blocks.shape, jnp.bfloat16),
-        in_specs=[pl.BlockSpec(memory_space=pltpu.SMEM), vmem, vmem, vmem, vmem],
+        in_specs=[pl.BlockSpec(memory_space=pltpu.SMEM), pl.BlockSpec(memory_space=pl.ANY), vmem, vmem, vmem],
         out_specs=vmem,
         scratch_shapes=[
+            pltpu.VMEM(wave_blocks.shape, jnp.bfloat16),
             pltpu.VMEM((classes, width, columns), jnp.float32),
             slots,
             slots,
             slots,
             slots,
+            pltpu.SemaphoreType.DMA((steps,)),
             pltpu.SemaphoreType.DMA((3, steps)),
             pltpu.SemaphoreType.DMA((3, steps)),
         ],

time: 300 us -> 298 us (level)
  no operation moved by 1% of the time
where the time goes in v4:
time: 298 us
  waiting for transfers between devices  142 us (48%)
  Pallas kernels  107 us (36%)
  local copies, waits for them, and re-layouts  33.4 us (11%)
  between operations  13.5 us (5%)
    all_gather x1, waiting for transfers between devices, per_device(): gathered = lax.all_gather(packed, 'bond', axis=0, tiled=True)  142 us
    pallas_call x1, Pallas kernels, per_device(): pl.pallas_call(functools.partial(contract_kernel, terms, width), out_shap...  107 us
    unnamed x11, local copies, waits for them, and re-layouts  9.77 us
    reshape x2, local copies, waits for them, and re-layouts, per_device(): left_env.reshape(sec_local, terms, width, width)  7.08 us
  transfers between devices with their start and end apart: 1, of which 1 were waited for; matrix products, arithmetic and copies ran while one was open for 4% of the time, Pallas kernels for 0%

profile of v4, /device:TPU:0, one launch (start us, length us, event | category | flops | bytes accessed | tf_op | source)
XLA Modules:
  0.0 297.5 jit_solution(12953297231489374261)
XLA Ops:
  6.5 3.8 %reshape.24 = bf16[32,5,64,64]{3,2,0,1:T(8,128)(2,1)S(1)} reshape(bf16[32,5,4096]{2,0,1:T(8,128)(2,1)} %param.8) | data formatting | bytes 2621440 | tf_op jit(solution)/shard_map/reshape | solution.py:13
  10.4 0.0 copy-start.1
  10.4 0.2 slice.8
  10.6 1.3 copy-done.1
  11.9 3.5 %copy.35 = bf16[32,2,64,2,64]{4,3,2,1,0:T(2,128)(2,1)} copy(bf16[32,2,64,2,64]{4,2,0,3,1:T(8,128)(2,1)S(1)} %bitcast.17) | data formatting | bytes 2097152 | tf_op jit(solution)/shard_map/transpose | solution.py:18
  15.4 3.9 %reshape.26 = bf16[32,128,128]{2,1,0:T(8,128)(2,1)S(1)} reshape(bf16[32,2,64,2,64]{4,3,2,1,0:T(2,128)(2,1)} %copy.35) | data formatting | bytes 2097152 | tf_op jit(solution)/shard_map/reshape | solution.py:18
  19.3 0.5 copy.36
  19.9 0.0 copy-start.3
  19.9 0.0 copy-start.2
  19.9 0.3 reshape.27
  20.2 1.2 pad_maximum_fusion
  21.3 0.0 all-gather.2.cloned.1.call-update
  21.4 0.1 copy.33
  21.5 0.1 constant_dynamic-slice_fusion
  21.6 0.1 copy.31
  21.6 0.7 reshape.21.sector_ref
  22.3 0.1 broadcast_in_dim.3
  22.4 0.7 broadcast_in_dim_reshape.4.gain_ref
  23.1 3.9 %reshape.22 = bf16[32,5,64,64]{3,2,0,1:T(8,128)(2,1)} reshape(bf16[32,5,4096]{2,0,1:T(8,128)(2,1)S(1)} %copy-done.2) | data formatting | bytes 2621440 | tf_op jit(solution)/shard_map/reshape | solution.py:175
  26.9 3.2 %copy.32 = bf16[32,5,64,64]{2,3,1,0:T(8,128)(2,1)S(1)} copy(bf16[32,5,64,64]{3,2,0,1:T(8,128)(2,1)} %reshape.22) | data formatting | bytes 2621440 | tf_op jit(solution)/shard_map/reshape | solution.py:175
  30.2 2.7 copy.37.left_ref
  32.9 142.2 %all-gather.2.cloned.1.call-done.right_ref = bf16[256,160,128]{2,1,0:T(8,128)(2,1)} async-done(((bf16[32,160,128]{2,1,0:T(8,128)(2,1)}), bf16[256,160,128]{2,1,0:T(8,128)(2,1)}) %all-gather.2.cloned.1.call-update) | async-done | bytes 10485776 | tf_op jit(solution)/shard_map/all_gather | solution.py:174
  175.1 107.1 %shard_map.64 = bf16[32,8,64,256]{3,2,1,0:T(8,128)(2,1)} custom-call(s32[256]{0:T(256)} %reshape.21.sector_ref, bf16[32,8,64,256]{3,2,1,0:T(8,128)(2,1)} %wave_hbm.1, bf16[32,64,320]{2,1,0:T(8,128)(2,1)} %copy.37.left_ref, f32[8,1,320]{2,1,0:T(1,128)} %broadcast_in_dim_reshape.4.gain_ref, bf16[256,160,128]{2,1,0:T(8,128)(2,1)} %all-gather.2.cloned.1.call-done.right_ref), custom_call_target="tpu_custom_call" | custom-call | tf_op jit(solution)/shard_map/pallas_call | solution.py:181
  282.2 8.4 %copy.41 = bf16[32,8,64,256]{3,2,1,0:T(8,128)(2,1)} copy(bf16[32,8,64,256]{3,2,1,0:T(8,128)(2,1)} %shard_map.64) | data formatting | bytes 16777216
  (10 shorter events, 0.0 us)
Async XLA Ops:
  6.5 15.0 %copy-start = (s32[256,8]{0,1:T(8,128)S(1)}, s32[256,8]{0,1:T(8,128)}, u32[]{:S(2)}) copy-start(s32[256,8]{0,1:T(8,128)} %param.11) | copy-start | bytes 24580
  6.5 168.5 %all-gather.2.cloned.1.call-start = ((), (), s32[]{:S(2)}) async-start(), calls=%async_computation | async-start | bytes 11796480 | tf_op jit(solution)/shard_map/all_gather | solution.py:174
  10.4 1.5 copy-start.1
  15.4 4.0 %slice-start = ((bf16[32,5,64,64]{3,2,0,1:T(8,128)(2,1)}), bf16[32,1,64,64]{3,2,0,1:T(8,128)(2,1)S(1)}, s32[]{:S(2)}) async-start(bf16[32,5,64,64]{3,2,0,1:T(8,128)(2,1)} %copy-done.1), calls=%async_computation.1 | async-start | bytes 1048576 | tf_op jit(solution)/shard_map/slice | solution.py:21
  19.9 1.5 copy-start.3
  19.9 1.5 copy-start.4
  19.9 3.2 %copy-start.2 = (bf16[32,5,4096]{2,0,1:T(8,128)(2,1)S(1)}, bf16[32,5,4096]{2,0,1:T(8,128)(2,1)}, u32[]{:S(2)}) copy-start(bf16[32,5,4096]{2,0,1:T(8,128)(2,1)} %param.7) | copy-start | bytes 3932164
Sparse Core Ops, SparseCore 0:
  21.5 153.5 all-gather.1
